TPU v7x, 32 devices: a whole 2x2x4 slice. The times are simulated.
32 devices in a mesh: comp: 2 (over core), rank: 16 (over z, y, x).
Axes of the slice: x: 2, y: 2, z: 4, core: 2. Of those that a mesh axis runs over, the one named last changes fastest.
Arguments:
- surface_fields: bfloat16 [2, 40, 65536], P('comp', None, 'rank'), may hold values from -6 to 6
- cell_area: float32 [2, 65536], P('comp', 'rank'), may hold values from 0.5 to 2
- remap_tiles: bfloat16 [2048, 128, 128], P('rank'), may hold values from -0.5 to 0.5
- pair_blocks: int32 [16, 16], P('rank'), may hold values from 0 to 8, as said below
- slot_cell: int32 [16, 16, 8], P('rank'), may hold values from 0 to 31
- node_block: int32 [16, 128], P('rank'), may hold values from 0 to 31
Outputs:
- surface_fluxes: float32 [2, 20, 65536], P('comp', None, 'rank')
Inputs may be any that keep to these rules, and one draw needn't show every extreme that they name: `pair_blocks`: entry [q, d] counts the live slots from atmosphere rank q to ocean rank d; in some rank's row every entry is 8.
All inputs are finite; a program needn't handle non-finite values.
Results may differ from a plain program's by a relative error of at most 0.0036.
Values may be sent and summed in bfloat16 or wider, within the bound.
No kernel may reach another device: no remote copies, remote signals or barrier semaphores. Data moves between devices by JAX's collectives and lax.ppermute only.
A program may use at most 128 MiB of HBM per device.

v0:
```python
import functools
import itertools
import math

import jax
import jax.numpy as jnp
from jax import lax
from jax.experimental import pallas as pl
from jax.experimental.pallas import tpu as pltpu
from jax.sharding import PartitionSpec as P

FLUX_IT = 5
DEVICES = ("comp", "rank")
SMEM = pl.BlockSpec(memory_space=pltpu.SMEM)
VMEM = pl.BlockSpec(memory_space=pltpu.VMEM)
ANY = pl.BlockSpec(memory_space=pl.ANY)
PARAMS = pltpu.CompilerParams(vmem_limit_bytes=24 << 20)


def swap_cores(value):
    return lax.ppermute(value, "comp", [(0, 1), (1, 0)])


def low_lanes(shape):
    return lax.broadcasted_iota(jnp.int32, shape, len(shape) - 1) < shape[-1] // 2


def half_turn(value):
    return pltpu.roll(value, value.shape[-1] // 2, value.ndim - 1)


def step_of(index, digit):
    return digit - 1 if index == 1 else max(index - 1, 0)


def peer_of(place, first, second, digit):
    return place[1] ^ jnp.where(place[0] == 0, first + digit * second, digit * first + second)


def tile_copies(digit, here, steps, tiles, held, sems):
    count = tiles.shape[0] // digit**2
    copies = []
    for at, (first, second) in enumerate(itertools.product(steps, range(digit))):
        peer = peer_of(here, first, second, digit)
        source = tiles.at[pl.ds(peer * count, count)]
        copies.append(
            pltpu.make_async_copy(source, held.at[at * count : (at + 1) * count], sems.at[at])
        )
    return copies


def load_kernel(digit, steps, tiles, counts, node_block, slot_cell, *refs):
    *held, place, kept, sems, tile_sems = refs
    here = lax.axis_index("comp"), lax.axis_index("rank")
    copies = [
        pltpu.make_async_copy(source, target, sems.at[i])
        for i, (source, target) in enumerate(
            zip((counts, node_block, slot_cell), held, strict=True)
        )
    ]
    copies += tile_copies(digit, here, steps, tiles, kept, tile_sems)
    for copy in copies:
        copy.start()
    place[0], place[1] = here
    for copy in copies:
        copy.wait()


def choose_kernel(place, mine, other, fields):
    @pl.when(place[0] == 0)
    def _():
        fields[...] = mine[...]

    @pl.when(place[0] == 1)
    def _():
        fields[...] = other[...]


def forward_kernel(digit, steps, place, counts, node_block, fields, tiles, *messages):
    field_rows, width = fields.shape[0], tiles.shape[2]
    pair_slots = node_block.shape[0] // digit**2
    low = low_lanes((field_rows, width))
    own = low == (place[0] == 0)
    for index, (message, first) in enumerate(zip(messages, steps, strict=True)):
        for second in range(digit):
            peer = peer_of(place, first, second, digit)
            tile = (index * digit + second) * pair_slots
            live = counts[peer]
            rows = []
            for slot in range(0, pair_slots, 2):
                at = peer * pair_slots + slot
                sources = []
                for i in range(2):
                    columns = pl.ds(pl.multiple_of(node_block[at + i] * width, width), width)
                    sources.append(fields[:, columns])
                products = jnp.dot(
                    jnp.concatenate(sources, axis=0),
                    jnp.concatenate([tiles[tile + slot], tiles[tile + slot + 1]], axis=1),
                    preferred_element_type=jnp.float32,
                )
                even = jnp.where(slot < live, products[:field_rows, :width], 0.0)
                odd = jnp.where(slot + 1 < live, products[field_rows:, width:], 0.0)
                turned = half_turn(jnp.where(low, odd, even))
                rows.append(jnp.where(own, jnp.where(low, even, odd), turned))
            message[second] = jnp.concatenate(rows, axis=0).astype(message.dtype)


def own_kernel(digit, place, counts, node_block, fields, tiles, message, held, sems):
    copies = tile_copies(digit, (place[0], place[1]), [0], tiles, held, sems)
    for copy in copies:
        copy.start()
    for copy in copies:
        copy.wait()
    forward_kernel(digit, [0], place, counts, node_block, fields, held, message)


def repack_kernel(*refs):
    digit = (len(refs) + 1) // 2
    held, out = refs[:digit], refs[digit:]
    for index in range(1, digit):
        for first in range(digit):
            out[index - 1][first] = held[first][step_of(index, digit)]


def turn_kernel(place, tiles, out, held, sem):
    copy = pltpu.make_async_copy(tiles, held, sem)
    copy.start()
    rank_count, pairs, width, _ = out.shape
    mid = width // 2
    copy.wait()
    for d in range(rank_count):
        for pair in range(pairs):
            for i in range(2):
                turned = held[(d * pairs + pair) * 2 + i].T
                out[d, pair, i * mid : (i + 1) * mid] = jnp.where(
                    place[0] == 0, turned[:mid], turned[mid:]
                )


def add_entries(message, slot_cell, source, even_sums, odd_sums):
    field_rows = even_sums.shape[1]
    rows = message.astype(jnp.float32)
    for slot in range(0, slot_cell.shape[0], 2):
        entry = rows[slot // 2 * field_rows : (slot // 2 + 1) * field_rows]
        even_sums[slot_cell[slot, source]] += entry
        odd_sums[slot_cell[slot + 1, source]] += entry


def early_kernel(place, slot_cell, mine, other, *refs):
    *held, even_sums, odd_sums, surface = refs
    digit = len(held)
    nblocks, field_rows, width = surface.shape
    ocean_core = place[0] == 1
    own = low_lanes((field_rows, width)) != ocean_core
    even_sums[...] = jnp.zeros_like(even_sums)
    odd_sums[...] = jnp.zeros_like(odd_sums)
    for index in range(digit):
        source = peer_of(place, step_of(index, digit), 0, digit)
        add_entries(held[index][0], slot_cell, source, even_sums, odd_sums)
    for block in range(nblocks):
        columns = slice(block * width, (block + 1) * width)
        values = jnp.where(ocean_core, mine[:, columns], other[:, columns]).astype(jnp.float32)
        surface[block] = jnp.where(own, values, half_turn(values))


def middle_kernel(index, digit, place, slot_cell, arrived, _, __, even_sums, odd_sums):
    for first in range(digit):
        source = peer_of(place, step_of(first, digit), step_of(index, digit), digit)
        add_entries(arrived[first], slot_cell, source, even_sums, odd_sums)


def ocean_kernel(digit, place, slot_cell, surface, own_area, other_area, arrived, *refs):
    _, _, sending, flux, even_sums, odd_sums, near, far, pull = refs
    nblocks, field_rows, width = surface.shape
    flux_rows = field_rows // 2
    pair_slots, rank_count = slot_cell.shape
    ocean_core = place[0] == 1

    middle_kernel(digit - 1, digit, place, slot_cell, arrived, None, None, even_sums, odd_sums)

    low = low_lanes((field_rows, width))
    for block in range(nblocks):
        mixed = jnp.where(low, even_sums[block], odd_sums[block])
        remapped = mixed + half_turn(mixed)
        near[block] = remapped[:flux_rows] - surface[block, :flux_rows]
        far[block] = (remapped * surface[block])[flux_rows:]

    wind_u, wind_v, excess = near[:, 0, :], near[:, 1, :], near[:, 2, :]
    wind_speed = jnp.sqrt(wind_u * wind_u + wind_v * wind_v + 0.25)
    stability = 1.0 + 4.0 * jax.nn.sigmoid(excess)
    transfer = jnp.ones_like(wind_speed)
    for sweep in range(FLUX_IT):
        transfer = 1.0 / (1.0 + stability * transfer)
    pull[...] = transfer * wind_speed

    own = low_lanes((flux_rows, width)) != ocean_core
    own_rows = low_lanes((nblocks, width)) != ocean_core
    area = jnp.where(ocean_core, own_area[...], other_area[...])
    area = jnp.where(own_rows, area, half_turn(area))
    for block in range(nblocks):
        value = pull[block : block + 1] * near[block] + far[block]
        flux[:, block, :] = jnp.where(own, value, 0.0)
        far[block] = value * area[block : block + 1]

    low = low[:flux_rows]
    for source in range(rank_count):
        rows = []
        for slot in range(0, pair_slots, 2):
            even, odd = slot_cell[slot, source], slot_cell[slot + 1, source]
            rows.append(jnp.where(low, far[even], far[odd]))
        sending[source] = jnp.concatenate(rows, axis=0).astype(sending.dtype)


def back_kernel(core, place, counts, node_block, pieces, turned, flux, out, *sums):
    rank_count, pairs, width, _ = turned.shape
    flux_rows, nblocks, _ = flux.shape
    span = sums[0].shape[1]
    low = low_lanes((span, width))

    @pl.when(place[0] != core)
    def _():
        out[...] = flux[...]

    @pl.when(place[0] == core)
    def _():
        for total in sums:
            total[...] = jnp.zeros_like(total)
        for d in range(rank_count):
            live = counts[d]
            rows = pieces[d].astype(jnp.float32)
            for pair in range(pairs):
                start = pair * flux_rows // 8 * 8
                piece = rows[start : start + span]
                halves = [jnp.where(low, piece, 0.0), jnp.where(low, 0.0, piece)]
                products = jnp.dot(
                    jnp.concatenate(halves, axis=0).astype(jnp.bfloat16),
                    turned[d, pair],
                    preferred_element_type=jnp.float32,
                )
                total = sums[(pair * flux_rows - start) // 4]
                for i in range(2):
                    slot = 2 * pair + i
                    block = node_block[d * 2 * pairs + slot]
                    block = jnp.where(slot < live, block, nblocks)
                    total[block] += products[i * span : (i + 1) * span]
        for k in range(flux_rows):
            nodes = sums[0][:nblocks, k, :]
            for i, total in enumerate(sums[1:], 1):
                nodes += total[:nblocks, k + 4 * i, :]
            out[k] = nodes


def on_device(surface_fields, cell_area, remap_tiles, pair_blocks, slot_cell, node_block):
    rank_count = lax.axis_size("rank")
    digit = math.isqrt(rank_count)
    fields = surface_fields[0]
    width = remap_tiles.shape[1]
    pair_slots = slot_cell.shape[2]
    pairs = pair_slots // 2
    field_rows, points = fields.shape
    flux_rows = field_rows // 2
    nblocks = points // width
    by_block = (nblocks, width)
    core = lax.axis_index("comp")

    def in_vmem(value):
        return pltpu.with_memory_space_constraint(value, pltpu.VMEM)

    def in_hbm(value):
        return pltpu.with_memory_space_constraint(value, pltpu.HBM)

    def call(kernel, name, in_specs, out_shape, scratch_shapes=(), **options):
        return pl.pallas_call(
            kernel,
            in_specs=in_specs,
            out_specs=jax.tree.map(lambda out: pl.BlockSpec(memory_space=out.memory_space), out_shape),
            out_shape=out_shape,
            scratch_shapes=scratch_shapes,
            compiler_params=PARAMS,
            name=name,
            **options,
        )

    def to_peer(value, phase, step):
        jumps = (step, step * digit) if phase == 0 else (step * digit, step)
        pairs = [
            (part * rank_count + rank, part * rank_count + (rank ^ jump))
            for part, jump in enumerate(jumps)
            for rank in range(rank_count)
        ]
        return in_vmem(lax.ppermute(value, DEVICES, pairs))

    other_fields = swap_cores(fields)
    other_area = swap_cores(cell_area)

    other_fields, other_area = lax.optimization_barrier((other_fields, other_area))

    def part(steps):
        count = len(steps) * digit
        return [
            pltpu.VMEM((count * pair_slots, width, width), jnp.bfloat16),
            pltpu.SemaphoreType.DMA((count,)),
        ]

    steps = [step_of(i, digit) for i in range(1, digit)]
    operands = [remap_tiles, pair_blocks[0], node_block[0], slot_cell[0].T]
    loaded, load_sems = part(steps)
    *tables, tiles = call(
        functools.partial(load_kernel, digit, steps),
        "load_tiles",
        [ANY] * 4,
        [pltpu.SMEM(table.shape, jnp.int32) for table in operands[1:]]
        + [pltpu.SMEM((2,), jnp.int32), loaded],
        [pltpu.SemaphoreType.DMA((3,)), load_sems],
    )(*map(in_hbm, operands))
    counts, slot_nodes, cells, place = [
        pltpu.with_memory_space_constraint(table, pltpu.SMEM) for table in tables
    ]

    blocks = pltpu.VMEM((digit, pair_slots // 2 * field_rows, width), jnp.bfloat16)
    atmosphere = call(
        choose_kernel, "atmosphere", [SMEM, VMEM, VMEM], pltpu.VMEM(fields.shape, jnp.bfloat16)
    )(place, fields, other_fields)

    messages = call(
        functools.partial(forward_kernel, digit, steps),
        "forward_products",
        [SMEM, SMEM, SMEM, VMEM, VMEM],
        [blocks] * len(steps),
    )(place, counts, slot_nodes, atmosphere, tiles)
    at_home = call(
        functools.partial(own_kernel, digit),
        "own_products",
        [SMEM, SMEM, SMEM, VMEM, ANY],
        blocks,
        part([0]),
    )(place, counts, slot_nodes, atmosphere, in_hbm(remap_tiles))
    brought = [to_peer(value, 0, step) for value, step in zip(messages, steps, strict=True)]
    held = [at_home] + brought
    onward = call(repack_kernel, "repack", [VMEM] * digit, [blocks] * (digit - 1))(*held)
    arrived = [to_peer(onward[i - 1], 1, step_of(i, digit)) for i in range(1, digit)]

    sums = pltpu.VMEM((nblocks, field_rows, width), jnp.float32)
    even_sums, odd_sums, surface = call(
        early_kernel, "early_sums", [SMEM, SMEM] + [VMEM] * (2 + digit), [sums] * 3
    )(place, cells, fields, other_fields, *held)

    turned_tiles, surface = lax.optimization_barrier((remap_tiles, surface))
    turned = call(
        turn_kernel,
        "turn_tiles",
        [SMEM, ANY],
        pltpu.VMEM((rank_count, pairs, width, width), jnp.bfloat16),
        [pltpu.VMEM(remap_tiles.shape, jnp.bfloat16), pltpu.SemaphoreType.DMA],
    )(place, in_hbm(turned_tiles))
    turned, surface = lax.optimization_barrier((turned, surface))

    by_flux = pltpu.VMEM((flux_rows, nblocks, width), jnp.float32)
    rows = pltpu.VMEM((nblocks, flux_rows, width), jnp.float32)
    for i, value in enumerate(arrived[:-1]):
        even_sums, odd_sums = call(
            functools.partial(middle_kernel, i + 1, digit),
            "middle_sums",
            [SMEM, SMEM, VMEM, VMEM, VMEM],
            [sums, sums],
            input_output_aliases={3: 0, 4: 1},
        )(place, cells, value, even_sums, odd_sums)
    sending, ocean_flux, _, _ = call(
        functools.partial(ocean_kernel, digit),
        "ocean_fluxes",
        [SMEM, SMEM] + [VMEM] * 6,
        [
            pltpu.VMEM((rank_count, pairs * flux_rows, width), jnp.bfloat16),
            by_flux,
            sums,
            sums,
        ],
        [rows, rows, pltpu.VMEM(by_block, jnp.float32)],
        input_output_aliases={6: 2, 7: 3},
    )(
        place,
        cells,
        surface,
        cell_area.reshape(by_block),
        other_area.reshape(by_block),
        arrived[-1],
        even_sums,
        odd_sums,
    )
    returned = lax.all_to_all(sending, "rank", split_axis=0, concat_axis=0, tiled=True)

    span = -(-flux_rows // 8) * 8

    def back(core, name, returned):
        return call(
            functools.partial(back_kernel, core),
            name,
            [SMEM, SMEM, SMEM, VMEM, VMEM, VMEM],
            by_flux,
            [pltpu.VMEM((nblocks + 1, span, width), jnp.float32)] * 2,
        )(place, counts, slot_nodes, in_vmem(returned), turned, ocean_flux)

    give = back(1, "given_sums", returned)
    returned, give = lax.optimization_barrier((returned, give))
    keep = back(0, "kept_sums", returned)
    divisor = jnp.where(core == 1, 1.0, cell_area.reshape(by_block))
    return ((keep + swap_cores(give)) / divisor).reshape(1, flux_rows, points)


def solution(mesh):
    return jax.shard_map(
        on_device,
        mesh=mesh,
        in_specs=(
            P("comp", None, "rank"),
            P("comp", "rank"),
            P("rank", None, None),
            P("rank", None),
            P("rank", None, None),
            P("rank", None),
        ),
        out_specs=P("comp", None, "rank"),
        check_vma=False,
    )
```

profile of v0, /device:TPU:0, one launch (start us, length us, event | category | flops | bytes accessed | tf_op | source)
XLA Modules:
  0.0 41.9 jit_solution(13184551389005593701)
XLA Ops:
  0.0 0.0 copy-start
  0.0 0.5 %collective-permute-start = (bf16[40,4096]{1,0:T(8,128)(2,1)}, bf16[40,4096]{1,0:T(8,128)(2,1)S(1)}, u32[]{:S(2)}, u32[]{:S(2)}) collective-permute-start(bf16[40,4096]{1,0:T(8,128)(2,1)} %bitcast.9), channel_id=1, source_target_pairs={{0,16},{16,0},{1,17},{17,1},{2,18},{18,2},{3,19},{19,3},{4,20},{20... | collective-permute-start | bytes 983048 | tf_op jit(solution)/shard_map/ppermute | solution.py:21
  0.5 0.1 collective-permute-start.1
  0.5 1.9 %load_tiles.1 = (s32[16]{0:T(128)S(4)}, s32[128]{0:T(128)S(4)}, s32[8,16]{1,0:T(8,128)S(4)}, s32[2]{0:T(128)S(4)}, bf16[96,128,128]{2,1,0:T(8,128)(2,1)S(1)}) custom-call(bf16[128,128,128]{2,1,0:T(8,128)(2,1)} %tiles.4, s32[16]{0:T(128)} %bitcast.16, s32[128]{0:T(128)} %bitcast.17, s32[8,16]{1,0:T(8,128)} %bitcast.15), custom_call_target="tpu_custom_call" | custom-call | tf_op jit(solution)/shard_map/load_tiles/pallas_call | solution.py:308
  2.5 0.0 collective-permute-done.1
  2.5 0.0 collective-permute-done.other
  2.5 0.0 copy-done
  2.5 0.8 %forward_products.1 = (bf16[4,160,128]{2,1,0:T(8,128)(2,1)S(1)}, bf16[4,160,128]{2,1,0:T(8,128)(2,1)S(1)}, bf16[4,160,128]{2,1,0:T(8,128)(2,1)S(1)}) custom-call(s32[2]{0:T(128)S(4)} %get-tuple-element.33.place, s32[16]{0:T(128)S(4)} %get-tuple-element.34.counts, s32[128]{0:T(128)S(4)} %get-tuple-element.35.node_block, ...), custom_call_target="tpu_custom_call" | custom-call | tf_op jit(solution)/shard_map/forward_products/pallas_call | solution.py:325
  3.4 3.9 %collective-permute-start.2 = (bf16[4,160,128]{2,1,0:T(8,128)(2,1)S(1)}, bf16[4,160,128]{2,1,0:T(8,128)(2,1)S(1)}, u32[]{:S(2)}, u32[]{:S(2)}) collective-permute-start(bf16[4,160,128]{2,1,0:T(8,128)(2,1)S(1)} %get-tuple-element.39), channel_id=1, source_target_pairs={{0,3},{1,2},{2,1},{3,0},{4,7},{5,6},{6,5},{7,4},{8,11},{9,10},{10,... | collective-permute-start | bytes 491528 | tf_op jit(solution)/shard_map/ppermute | solution.py:291
  7.3 0.5 %collective-permute-start.3 = (bf16[4,160,128]{2,1,0:T(8,128)(2,1)S(1)}, bf16[4,160,128]{2,1,0:T(8,128)(2,1)S(1)}, u32[]{:S(2)}, u32[]{:S(2)}) collective-permute-start(bf16[4,160,128]{2,1,0:T(8,128)(2,1)S(1)} %get-tuple-element.40), channel_id=1, source_target_pairs={{0,1},{1,0},{2,3},{3,2},{4,5},{5,4},{6,7},{7,6},{8,9},{9,8},{10,11... | collective-permute-start | bytes 491528 | tf_op jit(solution)/shard_map/ppermute | solution.py:291
  7.9 0.1 collective-permute-start.4
  8.0 1.6 %own_products.1.refs_0_ = bf16[4,160,128]{2,1,0:T(8,128)(2,1)S(1)} custom-call(s32[2]{0:T(128)S(4)} %get-tuple-element.33.place, s32[16]{0:T(128)S(4)} %get-tuple-element.34.counts, s32[128]{0:T(128)S(4)} %get-tuple-element.35.node_block, bf16[40,4096]{1,0:T(8,128)(2,1)S(1)} %atmosphere.1.fields, bf16[128,128,128]{2,1,0:T(8,128)(2,1)} %tiles.4), custom_call_target="tpu_custom_call" | custom-call | tf_op jit(solution)/shard_map/own_products/pallas_call | solution.py:331
  9.6 1.0 %collective-permute-done.2.refs_1_ = bf16[4,160,128]{2,1,0:T(8,128)(2,1)S(1)} collective-permute-done((bf16[4,160,128]{2,1,0:T(8,128)(2,1)S(1)}, bf16[4,160,128]{2,1,0:T(8,128)(2,1)S(1)}, u32[]{:S(2)}, u32[]{:S(2)}) %collective-permute-start.2) | collective-permute-done | bytes 163872 | tf_op jit(solution)/shard_map/ppermute | solution.py:291
  10.6 2.3 %collective-permute-done.3.refs_2_ = bf16[4,160,128]{2,1,0:T(8,128)(2,1)S(1)} collective-permute-done((bf16[4,160,128]{2,1,0:T(8,128)(2,1)S(1)}, bf16[4,160,128]{2,1,0:T(8,128)(2,1)S(1)}, u32[]{:S(2)}, u32[]{:S(2)}) %collective-permute-start.3) | collective-permute-done | bytes 163872 | tf_op jit(solution)/shard_map/ppermute | solution.py:291
  12.9 0.3 collective-permute-done.4.refs_3_
  13.2 3.7 %collective-permute-start.7 = (bf16[4,160,128]{2,1,0:T(8,128)(2,1)S(1)}, bf16[4,160,128]{2,1,0:T(8,128)(2,1)S(1)}, u32[]{:S(2)}, u32[]{:S(2)}) collective-permute-start(bf16[4,160,128]{2,1,0:T(8,128)(2,1)S(1)} %get-tuple-element.49), channel_id=1, source_target_pairs={{0,12},{1,13},{2,14},{3,15},{4,8},{5,9},{6,10},{7,11},{8,4},{9,5},... | collective-permute-start | bytes 491528 | tf_op jit(solution)/shard_map/ppermute | solution.py:291
  16.9 0.0 collective-permute-start.6
  16.9 0.8 %collective-permute-start.5 = (bf16[4,160,128]{2,1,0:T(8,128)(2,1)S(1)}, bf16[4,160,128]{2,1,0:T(8,128)(2,1)S(1)}, u32[]{:S(2)}, u32[]{:S(2)}) collective-permute-start(bf16[4,160,128]{2,1,0:T(8,128)(2,1)S(1)} %get-tuple-element.47), channel_id=1, source_target_pairs={{0,8},{1,9},{2,10},{3,11},{4,12},{5,13},{6,14},{7,15},{8,0},{9,1},... | collective-permute-start | bytes 491528 | tf_op jit(solution)/shard_map/ppermute | solution.py:291
  17.7 0.3 early_sums.1
  18.0 0.0 copy-start.1
  18.0 3.3 %turn_tiles.1.turned = bf16[16,4,128,128]{3,2,1,0:T(8,128)(2,1)S(1)} custom-call(s32[2]{0:T(128)S(4)} %get-tuple-element.33.place, bf16[128,128,128]{2,1,0:T(8,128)(2,1)} %tiles.4), custom_call_target="tpu_custom_call" | custom-call | tf_op jit(solution)/shard_map/turn_tiles/pallas_call | solution.py:349
  21.3 0.0 collective-permute-done.7.arrived
  21.3 0.1 middle_sums.2
  21.5 2.3 %collective-permute-done.6.arrived = bf16[4,160,128]{2,1,0:T(8,128)(2,1)S(1)} collective-permute-done((bf16[4,160,128]{2,1,0:T(8,128)(2,1)S(1)}, bf16[4,160,128]{2,1,0:T(8,128)(2,1)S(1)}, u32[]{:S(2)}, u32[]{:S(2)}) %collective-permute-start.6) | collective-permute-done | bytes 163872 | tf_op jit(solution)/shard_map/ppermute | solution.py:291
  23.8 0.1 middle_sums.3
  23.9 1.1 %collective-permute-done.5.arrived = bf16[4,160,128]{2,1,0:T(8,128)(2,1)S(1)} collective-permute-done((bf16[4,160,128]{2,1,0:T(8,128)(2,1)S(1)}, bf16[4,160,128]{2,1,0:T(8,128)(2,1)S(1)}, u32[]{:S(2)}, u32[]{:S(2)}) %collective-permute-start.5) | collective-permute-done | bytes 163872 | tf_op jit(solution)/shard_map/ppermute | solution.py:291
  24.9 0.0 copy-done.1
  24.9 0.9 %ocean_fluxes.1 = (bf16[16,80,128]{2,1,0:T(8,128)(2,1)S(1)}, f32[20,32,128]{2,1,0:T(8,128)S(1)}, f32[32,40,128]{2,1,0:T(8,128)S(1)}, f32[32,40,128]{2,1,0:T(8,128)S(1)}) custom-call(s32[2]{0:T(128)S(4)} %get-tuple-element.33.place, s32[8,16]{1,0:T(8,128)S(4)} %get-tuple-element.36.slot_cell, ...), custom_call_target="tpu_custom_call", output_to_operand_aliasing={{2}: (6, {}), {3}: (7, {})} | custom-call | tf_op jit(solution)/shard_map/ocean_fluxes/pallas_call | solution.py:368
  25.9 13.5 %all_to_all.5.pieces = bf16[16,80,128]{2,1,0:T(8,128)(2,1)S(1)} all-to-all(bf16[16,80,128]{2,1,0:T(8,128)(2,1)S(1)} %get-tuple-element.56), channel_id=1, replica_groups=mesh['comp'=2,'rank'=16] {'rank'}, dimensions={0} | all-to-all | bytes 655360 | tf_op jit(solution)/shard_map/all_to_all | solution.py:390
  39.4 0.1 collective-permute-start.8
  39.5 1.2 %kept_sums.1 = f32[20,32,128]{2,1,0:T(8,128)S(1)} custom-call(s32[2]{0:T(128)S(4)} %get-tuple-element.33.place, s32[16]{0:T(128)S(4)} %get-tuple-element.34.counts, s32[128]{0:T(128)S(4)} %get-tuple-element.35.node_block, bf16[16,80,128]{2,1,0:T(8,128)(2,1)S(1)} %all_to_all.5.pieces, bf16[16,4,128,128]{3,2,1,0:T(8,128)(2,1)S(1)} %turn_tiles.1.turned, ...), custom_call_target="tpu_custom_call" | custom-call | tf_op jit(solution)/shard_map/kept_sums/pallas_call | solution.py:395
  40.7 0.4 collective-permute-done.8
  41.1 0.8 %add_divide_fusion = f32[20,32,128]{2,1,0:T(8,128)} fusion(f32[20,32,128]{2,1,0:T(8,128)S(1)} %kept_sums.1, f32[20,32,128]{2,1,0:T(8,128)S(1)} %collective-permute-done.8, f32[32,128]{1,0:T(8,128)S(1)} %broadcast_select_fusion), kind=kLoop, calls=%fused_computation | loop fusion | flops 163840 | bytes 999424 | tf_op jit(solution)/shard_map/div | solution.py:407
  (4 shorter events, 0.1 us)
Async XLA Ops:
  0.0 2.5 %copy-start = (bf16[1,40,4096]{2,1,0:T(8,128)(2,1)S(1)}, bf16[1,40,4096]{2,1,0:T(8,128)(2,1)}, u32[]{:S(2)}) copy-start(bf16[1,40,4096]{2,1,0:T(8,128)(2,1)} %param.6) | copy-start | bytes 983044
  0.0 2.5 %collective-permute-start = (bf16[40,4096]{1,0:T(8,128)(2,1)}, bf16[40,4096]{1,0:T(8,128)(2,1)S(1)}, u32[]{:S(2)}, u32[]{:S(2)}) collective-permute-start(bf16[40,4096]{1,0:T(8,128)(2,1)} %bitcast.9), channel_id=1, source_target_pairs={{0,16},{16,0},{1,17},{17,1},{2,18},{18,2},{3,19},{19,3},{4,20},{20... | collective-permute-start | bytes 983048 | tf_op jit(solution)/shard_map/ppermute | solution.py:21
  0.5 2.0 %collective-permute-start.1 = (f32[1,4096]{1,0:T(1,128)}, f32[1,4096]{1,0:T(1,128)S(1)}, u32[]{:S(2)}, u32[]{:S(2)}) collective-permute-start(f32[1,4096]{1,0:T(1,128)} %param.7), channel_id=1, source_target_pairs={{0,16},{16,0},{1,17},{17,1},{2,18},{18,2},{3,19},{19,3},{4,20},{20... | collective-permute-start | bytes 49160 | tf_op jit(solution)/shard_map/ppermute | solution.py:21
  3.4 7.2 %collective-permute-start.2 = (bf16[4,160,128]{2,1,0:T(8,128)(2,1)S(1)}, bf16[4,160,128]{2,1,0:T(8,128)(2,1)S(1)}, u32[]{:S(2)}, u32[]{:S(2)}) collective-permute-start(bf16[4,160,128]{2,1,0:T(8,128)(2,1)S(1)} %get-tuple-element.39), channel_id=1, source_target_pairs={{0,3},{1,2},{2,1},{3,0},{4,7},{5,6},{6,5},{7,4},{8,11},{9,10},{10,... | collective-permute-start | bytes 491528 | tf_op jit(solution)/shard_map/ppermute | solution.py:291
  7.3 5.6 %collective-permute-start.3 = (bf16[4,160,128]{2,1,0:T(8,128)(2,1)S(1)}, bf16[4,160,128]{2,1,0:T(8,128)(2,1)S(1)}, u32[]{:S(2)}, u32[]{:S(2)}) collective-permute-start(bf16[4,160,128]{2,1,0:T(8,128)(2,1)S(1)} %get-tuple-element.40), channel_id=1, source_target_pairs={{0,1},{1,0},{2,3},{3,2},{4,5},{5,4},{6,7},{7,6},{8,9},{9,8},{10,11... | collective-permute-start | bytes 491528 | tf_op jit(solution)/shard_map/ppermute | solution.py:291
  7.9 5.3 %collective-permute-start.4 = (bf16[4,160,128]{2,1,0:T(8,128)(2,1)S(1)}, bf16[4,160,128]{2,1,0:T(8,128)(2,1)S(1)}, u32[]{:S(2)}, u32[]{:S(2)}) collective-permute-start(bf16[4,160,128]{2,1,0:T(8,128)(2,1)S(1)} %get-tuple-element.41), channel_id=1, source_target_pairs={{0,2},{1,3},{2,0},{3,1},{4,6},{5,7},{6,4},{7,5},{8,10},{9,11},{10,... | collective-permute-start | bytes 491528 | tf_op jit(solution)/shard_map/ppermute | solution.py:291
  13.2 8.1 %collective-permute-start.7 = (bf16[4,160,128]{2,1,0:T(8,128)(2,1)S(1)}, bf16[4,160,128]{2,1,0:T(8,128)(2,1)S(1)}, u32[]{:S(2)}, u32[]{:S(2)}) collective-permute-start(bf16[4,160,128]{2,1,0:T(8,128)(2,1)S(1)} %get-tuple-element.49), channel_id=1, source_target_pairs={{0,12},{1,13},{2,14},{3,15},{4,8},{5,9},{6,10},{7,11},{8,4},{9,5},... | collective-permute-start | bytes 491528 | tf_op jit(solution)/shard_map/ppermute | solution.py:291
  16.9 6.9 %collective-permute-start.6 = (bf16[4,160,128]{2,1,0:T(8,128)(2,1)S(1)}, bf16[4,160,128]{2,1,0:T(8,128)(2,1)S(1)}, u32[]{:S(2)}, u32[]{:S(2)}) collective-permute-start(bf16[4,160,128]{2,1,0:T(8,128)(2,1)S(1)} %get-tuple-element.48), channel_id=1, source_target_pairs={{0,4},{1,5},{2,6},{3,7},{4,0},{5,1},{6,2},{7,3},{8,12},{9,13},{10,... | collective-permute-start | bytes 491528 | tf_op jit(solution)/shard_map/ppermute | solution.py:291
  16.9 8.0 %collective-permute-start.5 = (bf16[4,160,128]{2,1,0:T(8,128)(2,1)S(1)}, bf16[4,160,128]{2,1,0:T(8,128)(2,1)S(1)}, u32[]{:S(2)}, u32[]{:S(2)}) collective-permute-start(bf16[4,160,128]{2,1,0:T(8,128)(2,1)S(1)} %get-tuple-element.47), channel_id=1, source_target_pairs={{0,8},{1,9},{2,10},{3,11},{4,12},{5,13},{6,14},{7,15},{8,0},{9,1},... | collective-permute-start | bytes 491528 | tf_op jit(solution)/shard_map/ppermute | solution.py:291
  18.0 7.0 %copy-start.1 = (f32[1,4096]{1,0:T(1,128)S(1)}, f32[1,4096]{1,0:T(1,128)}, u32[]{:S(2)}) copy-start(f32[1,4096]{1,0:T(1,128)} %param.7) | copy-start | bytes 49156
  39.4 1.7 %collective-permute-start.8 = (f32[20,32,128]{2,1,0:T(8,128)S(1)}, f32[20,32,128]{2,1,0:T(8,128)S(1)}, u32[]{:S(2)}, u32[]{:S(2)}) collective-permute-start(f32[20,32,128]{2,1,0:T(8,128)S(1)} %given_sums.1), channel_id=1, source_target_pairs={{0,16},{16,0},{1,17},{17,1},{2,18},{18,2},{3,19},{19,3},{4,20},{20... | collective-permute-start | bytes 983048 | tf_op jit(solution)/shard_map/ppermute | solution.py:21
where the time goes:
time: 42.1 us; the launch traced here: 41.9 us
  blocking collectives  13.5 us (32%)
  Pallas kernels  10.5 us (25%)
  starting transfers between devices  9.63 us (23%)
  waiting for transfers between devices  7.36 us (17%)
  other arithmetic  0.78 us (2%)
    all_to_all x1, blocking collectives, on_device(): lax.all_to_all(sending, 'rank', split_axis=0, concat_axis=0, tiled=True)  13.5 us
    ppermute x6, starting transfers between devices, to_peer(): return in_vmem(lax.ppermute(value, DEVICES, pairs))  9.04 us
    ppermute x6, waiting for transfers between devices, to_peer(): return in_vmem(lax.ppermute(value, DEVICES, pairs))  6.94 us
    pallas_call x1, Pallas kernels, on_device(): call(turn_kernel, 'turn_tiles', [SMEM, ANY], pltpu.VMEM((rank_count, pair...  3.34 us
    pallas_call x1, Pallas kernels, on_device(): call(functools.partial(load_kernel, digit, steps), 'load_tiles', [ANY] *...  1.95 us
    pallas_call x1, Pallas kernels, on_device(): call(functools.partial(own_kernel, digit), 'own_products', [SMEM, SMEM, S...  1.63 us
    pallas_call x2, Pallas kernels, back(): call(functools.partial(back_kernel, core), name, [SMEM, SMEM, SMEM, VMEM,...  1.21 us
    pallas_call x1, Pallas kernels, on_device(): call(functools.partial(ocean_kernel, digit), 'ocean_fluxes', [SMEM, SMEM]...  0.94 us
  transfers between devices with their start and end apart: 9, of which 6 were waited for; matrix products, arithmetic and copies ran while one was open for 0% of the time, Pallas kernels for 21%

commit v1 on v0

--- a/solution.py
+++ b/solution.py
@@ -219,7 +219,7 @@
 
     @pl.when(place[0] != core)
     def _():
-        out[...] = flux[...]
+        out[...] = flux[...].astype(out.dtype)
 
     @pl.when(place[0] == core)
     def _():
@@ -247,7 +247,7 @@
             nodes = sums[0][:nblocks, k, :]
             for i, total in enumerate(sums[1:], 1):
                 nodes += total[:nblocks, k + 4 * i, :]
-            out[k] = nodes
+            out[k] = nodes.astype(out.dtype)
 
 
 def on_device(surface_fields, cell_area, remap_tiles, pair_blocks, slot_cell, node_block):
@@ -391,20 +391,20 @@
 
     span = -(-flux_rows // 8) * 8
 
-    def back(core, name, returned):
+    def back(core, name, returned, out):
         return call(
             functools.partial(back_kernel, core),
             name,
             [SMEM, SMEM, SMEM, VMEM, VMEM, VMEM],
-            by_flux,
+            pltpu.VMEM(by_flux.shape, out),
             [pltpu.VMEM((nblocks + 1, span, width), jnp.float32)] * 2,
         )(place, counts, slot_nodes, in_vmem(returned), turned, ocean_flux)
 
-    give = back(1, "given_sums", returned)
+    give = back(1, "given_sums", returned, jnp.bfloat16)
     returned, give = lax.optimization_barrier((returned, give))
-    keep = back(0, "kept_sums", returned)
+    keep = back(0, "kept_sums", returned, jnp.float32)
     divisor = jnp.where(core == 1, 1.0, cell_area.reshape(by_block))
-    return ((keep + swap_cores(give)) / divisor).reshape(1, flux_rows, points)
+    return ((keep + swap_cores(give).astype(jnp.float32)) / divisor).reshape(1, flux_rows, points)
 
 
 def solution(mesh):

time: 42.1 us -> 42.8 us (1.017)
  blocking collectives: 13.5 us -> 0 us
  waiting for transfers between devices: 7.36 us -> 16.1 us
  starting transfers between devices: 9.63 us -> 14.3 us
  Pallas kernels: 10.5 us -> 11.2 us
    all_to_all x1 -> x0, blocking collectives: 13.5 us -> none  [on_device(): lax.all_to_all(sending, 'rank', split_axis=0, concat_axis=0, tiled=True)]
    all_to_all x0 -> x1, waiting for transfers between devices: none -> 9 us  [on_device(): lax.all_to_all(sending, 'rank', split_axis=0, concat_axis=0, tiled=True)]
    all_to_all x0 -> x1, starting transfers between devices: none -> 4.67 us  [on_device(): lax.all_to_all(sending, 'rank', split_axis=0, concat_axis=0, tiled=True)]
    pallas_call x1, Pallas kernels: 0.94 us -> 1.66 us  [on_device(): call(functools.partial(ocean_kernel, digit), 'ocean_fluxes', [SMEM, SMEM]...]
  transfers between devices with their start and end apart: 9 -> 10, of which waited for: 6 -> 7; matrix products, arithmetic and copies ran while one was open for 0% -> 0% of each run, Pallas kernels for 21% -> 20%
where the time goes in v1:
time: 42.8 us; the launch traced here: 42.5 us
  waiting for transfers between devices  16.1 us (38%)
  starting transfers between devices  14.3 us (33%)
  Pallas kernels  11.2 us (26%)
  other arithmetic  0.79 us (2%)
    ppermute x6, starting transfers between devices, to_peer(): return in_vmem(lax.ppermute(value, DEVICES, pairs))  9.04 us
    all_to_all x1, waiting for transfers between devices, on_device(): lax.all_to_all(sending, 'rank', split_axis=0, concat_axis=0, tiled=True)  9 us
    ppermute x6, waiting for transfers between devices, to_peer(): return in_vmem(lax.ppermute(value, DEVICES, pairs))  6.94 us
    all_to_all x1, starting transfers between devices, on_device(): lax.all_to_all(sending, 'rank', split_axis=0, concat_axis=0, tiled=True)  4.67 us
    pallas_call x1, Pallas kernels, on_device(): call(turn_kernel, 'turn_tiles', [SMEM, ANY], pltpu.VMEM((rank_count, pair...  3.34 us
    pallas_call x1, Pallas kernels, on_device(): call(functools.partial(load_kernel, digit, steps), 'load_tiles', [ANY] *...  1.95 us
    pallas_call x1, Pallas kernels, on_device(): call(functools.partial(ocean_kernel, digit), 'ocean_fluxes', [SMEM, SMEM]...  1.66 us
    pallas_call x1, Pallas kernels, on_device(): call(functools.partial(own_kernel, digit), 'own_products', [SMEM, SMEM, S...  1.64 us
  transfers between devices with their start and end apart: 10, of which 7 were waited for; matrix products, arithmetic and copies ran while one was open for 0% of the time, Pallas kernels for 20%

profile of v1, /device:TPU:0, one launch (start us, length us, event | category | flops | bytes accessed | tf_op | source)
XLA Modules:
  0.0 42.5 jit_solution(9233085329188157930)
XLA Ops:
  0.0 0.0 copy-start
  0.0 0.5 %collective-permute-start = (bf16[40,4096]{1,0:T(8,128)(2,1)}, bf16[40,4096]{1,0:T(8,128)(2,1)S(1)}, u32[]{:S(2)}, u32[]{:S(2)}) collective-permute-start(bf16[40,4096]{1,0:T(8,128)(2,1)} %bitcast.9), channel_id=1, source_target_pairs={{0,16},{16,0},{1,17},{17,1},{2,18},{18,2},{3,19},{19,3},{4,20},{20... | collective-permute-start | bytes 983048 | tf_op jit(solution)/shard_map/ppermute | solution.py:21
  0.5 0.1 collective-permute-start.1
  0.5 1.9 %load_tiles.1 = (s32[16]{0:T(128)S(4)}, s32[128]{0:T(128)S(4)}, s32[8,16]{1,0:T(8,128)S(4)}, s32[2]{0:T(128)S(4)}, bf16[96,128,128]{2,1,0:T(8,128)(2,1)S(1)}) custom-call(bf16[128,128,128]{2,1,0:T(8,128)(2,1)} %tiles.4, s32[16]{0:T(128)} %bitcast.16, s32[128]{0:T(128)} %bitcast.17, s32[8,16]{1,0:T(8,128)} %bitcast.15), custom_call_target="tpu_custom_call" | custom-call | tf_op jit(solution)/shard_map/load_tiles/pallas_call | solution.py:308
  2.5 0.0 collective-permute-done.1
  2.5 0.0 collective-permute-done.other
  2.5 0.0 copy-done
  2.5 0.8 %forward_products.1 = (bf16[4,160,128]{2,1,0:T(8,128)(2,1)S(1)}, bf16[4,160,128]{2,1,0:T(8,128)(2,1)S(1)}, bf16[4,160,128]{2,1,0:T(8,128)(2,1)S(1)}) custom-call(s32[2]{0:T(128)S(4)} %get-tuple-element.33.place, s32[16]{0:T(128)S(4)} %get-tuple-element.34.counts, s32[128]{0:T(128)S(4)} %get-tuple-element.35.node_block, ...), custom_call_target="tpu_custom_call" | custom-call | tf_op jit(solution)/shard_map/forward_products/pallas_call | solution.py:325
  3.4 3.9 %collective-permute-start.2 = (bf16[4,160,128]{2,1,0:T(8,128)(2,1)S(1)}, bf16[4,160,128]{2,1,0:T(8,128)(2,1)S(1)}, u32[]{:S(2)}, u32[]{:S(2)}) collective-permute-start(bf16[4,160,128]{2,1,0:T(8,128)(2,1)S(1)} %get-tuple-element.39), channel_id=1, source_target_pairs={{0,3},{1,2},{2,1},{3,0},{4,7},{5,6},{6,5},{7,4},{8,11},{9,10},{10,... | collective-permute-start | bytes 491528 | tf_op jit(solution)/shard_map/ppermute | solution.py:291
  7.3 0.5 %collective-permute-start.3 = (bf16[4,160,128]{2,1,0:T(8,128)(2,1)S(1)}, bf16[4,160,128]{2,1,0:T(8,128)(2,1)S(1)}, u32[]{:S(2)}, u32[]{:S(2)}) collective-permute-start(bf16[4,160,128]{2,1,0:T(8,128)(2,1)S(1)} %get-tuple-element.40), channel_id=1, source_target_pairs={{0,1},{1,0},{2,3},{3,2},{4,5},{5,4},{6,7},{7,6},{8,9},{9,8},{10,11... | collective-permute-start | bytes 491528 | tf_op jit(solution)/shard_map/ppermute | solution.py:291
  7.9 0.1 collective-permute-start.4
  8.0 1.6 %own_products.1.refs_0_ = bf16[4,160,128]{2,1,0:T(8,128)(2,1)S(1)} custom-call(s32[2]{0:T(128)S(4)} %get-tuple-element.33.place, s32[16]{0:T(128)S(4)} %get-tuple-element.34.counts, s32[128]{0:T(128)S(4)} %get-tuple-element.35.node_block, bf16[40,4096]{1,0:T(8,128)(2,1)S(1)} %atmosphere.1.fields, bf16[128,128,128]{2,1,0:T(8,128)(2,1)} %tiles.4), custom_call_target="tpu_custom_call" | custom-call | tf_op jit(solution)/shard_map/own_products/pallas_call | solution.py:331
  9.6 1.0 %collective-permute-done.2.refs_1_ = bf16[4,160,128]{2,1,0:T(8,128)(2,1)S(1)} collective-permute-done((bf16[4,160,128]{2,1,0:T(8,128)(2,1)S(1)}, bf16[4,160,128]{2,1,0:T(8,128)(2,1)S(1)}, u32[]{:S(2)}, u32[]{:S(2)}) %collective-permute-start.2) | collective-permute-done | bytes 163872 | tf_op jit(solution)/shard_map/ppermute | solution.py:291
  10.6 2.3 %collective-permute-done.3.refs_2_ = bf16[4,160,128]{2,1,0:T(8,128)(2,1)S(1)} collective-permute-done((bf16[4,160,128]{2,1,0:T(8,128)(2,1)S(1)}, bf16[4,160,128]{2,1,0:T(8,128)(2,1)S(1)}, u32[]{:S(2)}, u32[]{:S(2)}) %collective-permute-start.3) | collective-permute-done | bytes 163872 | tf_op jit(solution)/shard_map/ppermute | solution.py:291
  12.9 0.3 collective-permute-done.4.refs_3_
  13.2 3.7 %collective-permute-start.7 = (bf16[4,160,128]{2,1,0:T(8,128)(2,1)S(1)}, bf16[4,160,128]{2,1,0:T(8,128)(2,1)S(1)}, u32[]{:S(2)}, u32[]{:S(2)}) collective-permute-start(bf16[4,160,128]{2,1,0:T(8,128)(2,1)S(1)} %get-tuple-element.49), channel_id=1, source_target_pairs={{0,12},{1,13},{2,14},{3,15},{4,8},{5,9},{6,10},{7,11},{8,4},{9,5},... | collective-permute-start | bytes 491528 | tf_op jit(solution)/shard_map/ppermute | solution.py:291
  16.9 0.0 collective-permute-start.6
  16.9 0.8 %collective-permute-start.5 = (bf16[4,160,128]{2,1,0:T(8,128)(2,1)S(1)}, bf16[4,160,128]{2,1,0:T(8,128)(2,1)S(1)}, u32[]{:S(2)}, u32[]{:S(2)}) collective-permute-start(bf16[4,160,128]{2,1,0:T(8,128)(2,1)S(1)} %get-tuple-element.47), channel_id=1, source_target_pairs={{0,8},{1,9},{2,10},{3,11},{4,12},{5,13},{6,14},{7,15},{8,0},{9,1},... | collective-permute-start | bytes 491528 | tf_op jit(solution)/shard_map/ppermute | solution.py:291
  17.7 0.3 early_sums.1
  18.0 0.0 copy-start.1
  18.0 3.3 %turn_tiles.1.turned = bf16[16,4,128,128]{3,2,1,0:T(8,128)(2,1)S(1)} custom-call(s32[2]{0:T(128)S(4)} %get-tuple-element.33.place, bf16[128,128,128]{2,1,0:T(8,128)(2,1)} %tiles.4), custom_call_target="tpu_custom_call" | custom-call | tf_op jit(solution)/shard_map/turn_tiles/pallas_call | solution.py:349
  21.3 0.0 collective-permute-done.7.arrived
  21.3 0.1 middle_sums.2
  21.5 2.3 %collective-permute-done.6.arrived = bf16[4,160,128]{2,1,0:T(8,128)(2,1)S(1)} collective-permute-done((bf16[4,160,128]{2,1,0:T(8,128)(2,1)S(1)}, bf16[4,160,128]{2,1,0:T(8,128)(2,1)S(1)}, u32[]{:S(2)}, u32[]{:S(2)}) %collective-permute-start.6) | collective-permute-done | bytes 163872 | tf_op jit(solution)/shard_map/ppermute | solution.py:291
  23.8 0.1 middle_sums.3
  23.9 1.1 %collective-permute-done.5.arrived = bf16[4,160,128]{2,1,0:T(8,128)(2,1)S(1)} collective-permute-done((bf16[4,160,128]{2,1,0:T(8,128)(2,1)S(1)}, bf16[4,160,128]{2,1,0:T(8,128)(2,1)S(1)}, u32[]{:S(2)}, u32[]{:S(2)}) %collective-permute-start.5) | collective-permute-done | bytes 163872 | tf_op jit(solution)/shard_map/ppermute | solution.py:291
  24.9 0.0 copy-done.1
  24.9 1.7 %ocean_fluxes.1 = (bf16[16,80,128]{2,1,0:T(8,128)(2,1)}, f32[20,32,128]{2,1,0:T(8,128)S(1)}, f32[32,40,128]{2,1,0:T(8,128)S(1)}, f32[32,40,128]{2,1,0:T(8,128)S(1)}) custom-call(s32[2]{0:T(128)S(4)} %get-tuple-element.33.place, s32[8,16]{1,0:T(8,128)S(4)} %get-tuple-element.36.slot_cell, ...), custom_call_target="tpu_custom_call", output_to_operand_aliasing={{2}: (6, {}), {3}: (7, {})} | custom-call | tf_op jit(solution)/shard_map/ocean_fluxes/pallas_call | solution.py:368
  26.6 4.7 %all-to-all-start = ((bf16[16,80,128]{2,1,0:T(8,128)(2,1)}), bf16[16,80,128]{2,1,0:T(8,128)(2,1)S(1)}, u32[]{:S(2)}, u32[]{:S(2)}) async-start(bf16[16,80,128]{2,1,0:T(8,128)(2,1)} %get-tuple-element.56), calls=%async_computation | async-start | bytes 655360 | tf_op jit(solution)/shard_map/all_to_all | solution.py:390
  31.3 9.0 %all-to-all-done.pieces = bf16[16,80,128]{2,1,0:T(8,128)(2,1)S(1)} async-done(((bf16[16,80,128]{2,1,0:T(8,128)(2,1)}), bf16[16,80,128]{2,1,0:T(8,128)(2,1)S(1)}, u32[]{:S(2)}, u32[]{:S(2)}) %all-to-all-start) | async-done | bytes 327712 | tf_op jit(solution)/shard_map/all_to_all | solution.py:390
  40.3 0.1 collective-permute-start.8
  40.4 1.2 %kept_sums.1 = f32[20,32,128]{2,1,0:T(8,128)S(1)} custom-call(s32[2]{0:T(128)S(4)} %get-tuple-element.33.place, s32[16]{0:T(128)S(4)} %get-tuple-element.34.counts, s32[128]{0:T(128)S(4)} %get-tuple-element.35.node_block, bf16[16,80,128]{2,1,0:T(8,128)(2,1)S(1)} %all-to-all-done.pieces, bf16[16,4,128,128]{3,2,1,0:T(8,128)(2,1)S(1)} %turn_tiles.1.turned, ...), custom_call_target="tpu_custom_call" | custom-call | tf_op jit(solution)/shard_map/kept_sums/pallas_call | solution.py:395
  41.6 0.2 collective-permute-done.8
  41.8 0.8 %add_divide_fusion = f32[20,32,128]{2,1,0:T(8,128)} fusion(f32[20,32,128]{2,1,0:T(8,128)S(1)} %kept_sums.1, bf16[20,32,128]{2,1,0:T(8,128)(2,1)S(1)} %collective-permute-done.8, f32[32,128]{1,0:T(8,128)S(1)} %broadcast_select_fusion), kind=kLoop, calls=%fused_computation | loop fusion | flops 245760 | bytes 835584 | tf_op jit(solution)/shard_map/div | solution.py:407
  (4 shorter events, 0.1 us)
Async XLA Ops:
  0.0 2.5 %copy-start = (bf16[1,40,4096]{2,1,0:T(8,128)(2,1)S(1)}, bf16[1,40,4096]{2,1,0:T(8,128)(2,1)}, u32[]{:S(2)}) copy-start(bf16[1,40,4096]{2,1,0:T(8,128)(2,1)} %param.6) | copy-start | bytes 983044
  0.0 2.5 %collective-permute-start = (bf16[40,4096]{1,0:T(8,128)(2,1)}, bf16[40,4096]{1,0:T(8,128)(2,1)S(1)}, u32[]{:S(2)}, u32[]{:S(2)}) collective-permute-start(bf16[40,4096]{1,0:T(8,128)(2,1)} %bitcast.9), channel_id=1, source_target_pairs={{0,16},{16,0},{1,17},{17,1},{2,18},{18,2},{3,19},{19,3},{4,20},{20... | collective-permute-start | bytes 983048 | tf_op jit(solution)/shard_map/ppermute | solution.py:21
  0.5 2.0 %collective-permute-start.1 = (f32[1,4096]{1,0:T(1,128)}, f32[1,4096]{1,0:T(1,128)S(1)}, u32[]{:S(2)}, u32[]{:S(2)}) collective-permute-start(f32[1,4096]{1,0:T(1,128)} %param.7), channel_id=1, source_target_pairs={{0,16},{16,0},{1,17},{17,1},{2,18},{18,2},{3,19},{19,3},{4,20},{20... | collective-permute-start | bytes 49160 | tf_op jit(solution)/shard_map/ppermute | solution.py:21
  3.4 7.2 %collective-permute-start.2 = (bf16[4,160,128]{2,1,0:T(8,128)(2,1)S(1)}, bf16[4,160,128]{2,1,0:T(8,128)(2,1)S(1)}, u32[]{:S(2)}, u32[]{:S(2)}) collective-permute-start(bf16[4,160,128]{2,1,0:T(8,128)(2,1)S(1)} %get-tuple-element.39), channel_id=1, source_target_pairs={{0,3},{1,2},{2,1},{3,0},{4,7},{5,6},{6,5},{7,4},{8,11},{9,10},{10,... | collective-permute-start | bytes 491528 | tf_op jit(solution)/shard_map/ppermute | solution.py:291
  7.3 5.6 %collective-permute-start.3 = (bf16[4,160,128]{2,1,0:T(8,128)(2,1)S(1)}, bf16[4,160,128]{2,1,0:T(8,128)(2,1)S(1)}, u32[]{:S(2)}, u32[]{:S(2)}) collective-permute-start(bf16[4,160,128]{2,1,0:T(8,128)(2,1)S(1)} %get-tuple-element.40), channel_id=1, source_target_pairs={{0,1},{1,0},{2,3},{3,2},{4,5},{5,4},{6,7},{7,6},{8,9},{9,8},{10,11... | collective-permute-start | bytes 491528 | tf_op jit(solution)/shard_map/ppermute | solution.py:291
  7.9 5.3 %collective-permute-start.4 = (bf16[4,160,128]{2,1,0:T(8,128)(2,1)S(1)}, bf16[4,160,128]{2,1,0:T(8,128)(2,1)S(1)}, u32[]{:S(2)}, u32[]{:S(2)}) collective-permute-start(bf16[4,160,128]{2,1,0:T(8,128)(2,1)S(1)} %get-tuple-element.41), channel_id=1, source_target_pairs={{0,2},{1,3},{2,0},{3,1},{4,6},{5,7},{6,4},{7,5},{8,10},{9,11},{10,... | collective-permute-start | bytes 491528 | tf_op jit(solution)/shard_map/ppermute | solution.py:291
  13.2 8.1 %collective-permute-start.7 = (bf16[4,160,128]{2,1,0:T(8,128)(2,1)S(1)}, bf16[4,160,128]{2,1,0:T(8,128)(2,1)S(1)}, u32[]{:S(2)}, u32[]{:S(2)}) collective-permute-start(bf16[4,160,128]{2,1,0:T(8,128)(2,1)S(1)} %get-tuple-element.49), channel_id=1, source_target_pairs={{0,12},{1,13},{2,14},{3,15},{4,8},{5,9},{6,10},{7,11},{8,4},{9,5},... | collective-permute-start | bytes 491528 | tf_op jit(solution)/shard_map/ppermute | solution.py:291
  16.9 6.9 %collective-permute-start.6 = (bf16[4,160,128]{2,1,0:T(8,128)(2,1)S(1)}, bf16[4,160,128]{2,1,0:T(8,128)(2,1)S(1)}, u32[]{:S(2)}, u32[]{:S(2)}) collective-permute-start(bf16[4,160,128]{2,1,0:T(8,128)(2,1)S(1)} %get-tuple-element.48), channel_id=1, source_target_pairs={{0,4},{1,5},{2,6},{3,7},{4,0},{5,1},{6,2},{7,3},{8,12},{9,13},{10,... | collective-permute-start | bytes 491528 | tf_op jit(solution)/shard_map/ppermute | solution.py:291
  16.9 8.0 %collective-permute-start.5 = (bf16[4,160,128]{2,1,0:T(8,128)(2,1)S(1)}, bf16[4,160,128]{2,1,0:T(8,128)(2,1)S(1)}, u32[]{:S(2)}, u32[]{:S(2)}) collective-permute-start(bf16[4,160,128]{2,1,0:T(8,128)(2,1)S(1)} %get-tuple-element.47), channel_id=1, source_target_pairs={{0,8},{1,9},{2,10},{3,11},{4,12},{5,13},{6,14},{7,15},{8,0},{9,1},... | collective-permute-start | bytes 491528 | tf_op jit(solution)/shard_map/ppermute | solution.py:291
  18.0 7.0 %copy-start.1 = (f32[1,4096]{1,0:T(1,128)S(1)}, f32[1,4096]{1,0:T(1,128)}, u32[]{:S(2)}) copy-start(f32[1,4096]{1,0:T(1,128)} %param.7) | copy-start | bytes 49156
  26.6 13.7 %all-to-all-start = ((bf16[16,80,128]{2,1,0:T(8,128)(2,1)}), bf16[16,80,128]{2,1,0:T(8,128)(2,1)S(1)}, u32[]{:S(2)}, u32[]{:S(2)}) async-start(bf16[16,80,128]{2,1,0:T(8,128)(2,1)} %get-tuple-element.56), calls=%async_computation | async-start | bytes 655360 | tf_op jit(solution)/shard_map/all_to_all | solution.py:390
  40.3 1.5 %collective-permute-start.8 = (bf16[20,32,128]{2,1,0:T(8,128)(2,1)S(1)}, bf16[20,32,128]{2,1,0:T(8,128)(2,1)S(1)}, u32[]{:S(2)}, u32[]{:S(2)}) collective-permute-start(bf16[20,32,128]{2,1,0:T(8,128)(2,1)S(1)} %given_sums.1), channel_id=1, source_target_pairs={{0,16},{16,0},{1,17},{17,1},{2,18},{18,2},{3,19},{19,3},{4,20},{20... | collective-permute-start | bytes 491528 | tf_op jit(solution)/shard_map/ppermute | solution.py:21
